TPU v7x, 256 devices: a whole 4x4x8 slice. The times are simulated.
256 devices in a mesh: row: 16 (over x, y_lo, core), col: 16 (over z, y_hi).
Axes of the slice: x: 4, y: 4 (y_hi: 2, y_lo: 2; y = y_hi * 2 + y_lo), z: 8, core: 2. Of those that a mesh axis runs over, the one named last changes fastest.
Arguments:
- embeddings: bfloat16 [49152, 128], P(('row', 'col')), as said below
- recordings: int32 [49152], P(('row', 'col')), may hold values from 0 to 6143
- start_basis: bfloat16 [32, 49152], P(None, ('row', 'col')), may hold values from -6 to 6
Outputs:
- basis: float32 [32, 49152], P(None, ('row', 'col'))
Inputs may be any that keep to these rules, and one draw needn't show every extreme that they name: `embeddings`: one embedding per speaker segment.
All inputs are finite; a program needn't handle non-finite values.
Results may differ from a plain program's by a relative error of at most 0.0057.
Values may be sent and summed in bfloat16 or wider, within the bound.
A program may use at most 64 MiB of HBM per device.

v0:
```python
import math

import jax
import jax.numpy as jnp
from jax import lax
from jax.sharding import PartitionSpec as P


def unit_rows(embeddings):
    values = embeddings.astype(jnp.float32)
    width = values.shape[1]
    scale = lax.rsqrt(jnp.mean(values * values, axis=1, keepdims=True) + 1e-06) / math.sqrt(width)
    return (values * scale).astype(jnp.bfloat16)


def affinity_of(cosine, same_rec, width):
    tau_value = 2.5 / math.sqrt(width)
    beta_value = 2.0 * math.sqrt(width)
    weights = jnp.maximum(jnp.exp(beta_value * (cosine - tau_value)) - 1.0, 0.0)
    return jnp.where(same_rec, jnp.zeros_like(weights), weights)


def on_device(embeddings, recordings, start_basis):
    seg_len = embeddings.shape[0]
    width = embeddings.shape[1]
    ncols = lax.axis_size("col")
    nrows = lax.axis_size("row")
    units_own = unit_rows(embeddings)
    row_units, row_ids = (
        lax.all_gather(units_own, "col", axis=0, tiled=True),
        lax.all_gather(recordings, "col", axis=0, tiled=True),
    )
    col_units, col_ids, col_basis = (
        lax.all_gather(units_own, "row", axis=0, tiled=True),
        lax.all_gather(recordings, "row", axis=0, tiled=True),
        lax.all_gather(start_basis, "row", axis=1, tiled=True),
    )
    row_count = row_units.shape[0]
    col_count = col_units.shape[0]
    group_size = 1
    for divisor in range(1, ncols + 1):
        if ncols % divisor == 0 and seg_len * divisor <= 512:
            group_size = divisor
    block_len = seg_len * group_size
    block_count = row_count // block_len
    unit_blocks = row_units.reshape(block_count, block_len, width)
    id_blocks = row_ids.reshape(block_count, block_len)

    def weight_tile(units_block, ids_block):
        cosine = jnp.dot(units_block, col_units.T, preferred_element_type=jnp.float32)
        return affinity_of(cosine, ids_block[:, None] == col_ids[None, :], width)

    col_start = lax.axis_index("col") * seg_len

    def first_pass(carry, inputs):
        weights = weight_tile(inputs[0], inputs[1])
        return (
            carry + jnp.sum(weights, axis=0),
            (jnp.sum(weights, axis=1), weights.astype(jnp.bfloat16)),
        )

    col_sums, (row_sums, tiles) = lax.scan(
        first_pass, jnp.zeros((col_count,), jnp.float32), (unit_blocks, id_blocks)
    )
    row_degree = 1.0 + lax.psum(row_sums.reshape(row_count), "col")
    col_degree = 1.0 + lax.psum(col_sums, "row")
    scaled = (col_basis.astype(jnp.float32) * lax.rsqrt(col_degree)[None, :]).astype(jnp.bfloat16)
    parts = jnp.einsum("kc,blc->kbl", scaled, tiles, preferred_element_type=jnp.float32)
    partial_image = parts.reshape(parts.shape[0], row_count)
    owned = lax.psum_scatter(partial_image, "col", scatter_dimension=1, tiled=True)
    own_degree_rows = lax.dynamic_slice_in_dim(row_degree, col_start, seg_len, 0)
    image_rows = owned * lax.rsqrt(own_degree_rows)[None, :]
    gram = lax.psum(
        jnp.dot(image_rows, image_rows.T, precision=lax.Precision.HIGHEST), ("row", "col")
    )
    factor_low = jnp.linalg.cholesky(gram)
    solved = jax.scipy.linalg.solve_triangular(factor_low, image_rows, lower=True)
    return solved * math.sqrt(seg_len * nrows * ncols)


def solution(mesh):
    in_specs = (P(("row", "col"), None), P(("row", "col")), P(None, ("row", "col")))
    out_specs = P(None, ("row", "col"))
    return jax.shard_map(
        on_device, mesh=mesh, in_specs=in_specs, out_specs=out_specs, check_vma=False
    )
```

profile of v0, /device:TPU:1, one launch (start us, length us, event | category | flops | bytes accessed | tf_op | source)
XLA Modules:
  0.0 620.6 jit_solution(2310686160275048345)
XLA Ops:
  6.5 0.9 fusion.7
  7.5 0.9 fusion.8
  8.4 42.2 %all_gather.18 = bf16[3072,128]{1,0:T(8,128)(2,1)S(1)} all-gather(bf16[192,128]{1,0:T(8,128)(2,1)S(1)} %fusion.8), channel_id=1, replica_groups=mesh['row'=16,'col'=16] {'col'}, dimensions={0}, use_global_device_ids=true | all-gather | bytes 835584 | tf_op jit(solution)/shard_map/all_gather | solution.py:30
  50.6 30.0 %all_gather.19 = bf16[3072,128]{1,0:T(8,128)(2,1)} all-gather(bf16[192,128]{1,0:T(8,128)(2,1)S(1)} %fusion.8), channel_id=1, replica_groups=mesh['row'=16,'col'=16] {'row'}, dimensions={0}, use_global_device_ids=true | all-gather | bytes 835584 | tf_op jit(solution)/shard_map/all_gather | solution.py:34
  80.6 1.3 dynamic-slice
  82.5 0.9 dynamic-update-slice.3
  83.3 58.2 %all-reduce = s32[3072]{0:T(1024)S(1)} all-reduce(s32[3072]{0:T(1024)S(1)} %dynamic-update-slice.3), channel_id=1, replica_groups=mesh['row'=16,'col'=16] {'col'}, use_global_device_ids=true, to_apply=%add | all-reduce | flops 3072 | bytes 24576
  141.6 1.3 dynamic-slice.1
  143.4 0.9 dynamic-update-slice.4
  144.3 62.4 %all-reduce.1 = s32[3072]{0:T(1024)S(1)} all-reduce(s32[3072]{0:T(1024)S(1)} %dynamic-update-slice.4), channel_id=1, replica_groups=mesh['row'=16,'col'=16] {'row'}, use_global_device_ids=true, to_apply=%add.1 | all-reduce | flops 3072 | bytes 24576
  206.7 38.6 %while.17 = (s32[]{:T(128)}, f32[3072]{0:T(1024)S(1)}, f32[8,384]{1,0:T(8,128)S(1)}, bf16[8,384,3072]{2,1,0:T(8,128)(2,1)}, s32[8,384]{1,0:T(8,128)S(1)}, /*inde...) while((s32[]{:T(128)}, f32[3072]{0:T(1024)S(1)}, ...), condition=%wide.region_4.5_spmd.clone, body=%wide.region_1.4_spmd.clone.sunk | while | flops 312609408 | bytes 8036999 | solution.py:62
  206.7 3.1 fusion.24
  209.9 0.1 dynamic_update_slice.20
  209.9 1.6 bitcast_dynamic-update-slice_fusion.2
  211.5 3.1 fusion.24
  214.7 0.1 dynamic_update_slice.20
  214.8 1.5 bitcast_dynamic-update-slice_fusion.2
  216.3 3.1 fusion.24
  219.5 0.1 dynamic_update_slice.20
  219.5 1.6 bitcast_dynamic-update-slice_fusion.2
  221.2 3.1 fusion.24
  224.3 0.1 dynamic_update_slice.20
  224.4 1.6 bitcast_dynamic-update-slice_fusion.2
  226.0 3.1 fusion.24
  229.2 1.6 bitcast_dynamic-update-slice_fusion.2
  230.8 3.1 fusion.24
  234.0 1.7 bitcast_dynamic-update-slice_fusion.2
  235.7 3.1 fusion.24
  238.9 1.6 bitcast_dynamic-update-slice_fusion.2
  240.5 3.1 fusion.24
  243.7 1.6 bitcast_dynamic-update-slice_fusion.2
  245.3 20.9 %all-gather = bf16[16,192,32]{1,2,0:T(8,128)(2,1)S(1)} all-gather(bf16[1,192,32]{1,2,0:T(8,128)(2,1)S(1)} %bitcast.42), channel_id=1, replica_groups=mesh['row'=16,'col'=16] {'row'}, dimensions={0}, use_global_device_ids=true | all-gather | bytes 208896 | tf_op jit(solution)/shard_map/all_gather | solution.py:36
  266.2 0.2 copy.10
  266.4 0.2 reshape.53
  266.6 50.4 %psum.21 = f32[3072]{0:T(1024)S(1)} all-reduce(f32[3072]{0:T(1024)S(1)} %get-tuple-element.109), channel_id=1, replica_groups=mesh['row'=16,'col'=16] {'row'}, use_global_device_ids=true, to_apply=%region_5.6 | all-reduce | flops 3072 | bytes 24576 | tf_op jit(solution)/shard_map/psum | solution.py:66
  317.0 10.1 %fusion.4 = f32[32,8,384]{0,2,1:T(8,128)} fusion(bf16[8,384,3072]{2,1,0:T(8,128)(2,1)} %get-tuple-element.110, f32[3072,32]{0,1:T(8,128)S(1)} %reshape.53, f32[3072]{0:T(1024)S(1)} %add_rsqrt_fusion), kind=kOutput, calls=%fused_computation.10 | convolution fusion | flops 604176384 | bytes 19673088
  327.2 58.9 %psum.22 = f32[3072]{0:T(1024)S(1)} all-reduce(f32[3072]{0:T(1024)S(1)} %reshape.40), channel_id=1, replica_groups=mesh['row'=16,'col'=16] {'col'}, use_global_device_ids=true, to_apply=%region_7.8 | all-reduce | flops 3072 | bytes 24576 | tf_op jit(solution)/shard_map/psum | solution.py:65
  386.0 0.1 fusion.17
  386.1 139.4 %reduce-scatter.4.cloned.1.call-done = f32[192,32]{1,0:T(8,128)} async-done(((f32[3072,32]{1,0:T(8,128)}), f32[192,32]{1,0:T(8,128)}) %reduce-scatter.4.cloned.1.call-update) | async-done | bytes 24592
  525.5 1.0 copy.16
  526.4 0.2 fusion.10
  526.6 79.5 %psum.23 = f32[32,32]{0,1:T(8,128)S(1)} all-reduce(f32[32,32]{0,1:T(8,128)S(1)} %fusion.10), channel_id=1, replica_groups=mesh['row'=16,'col'=16] {'row','col'}, use_global_device_ids=true, to_apply=%region_8.9 | all-reduce | flops 1024 | bytes 8192 | tf_op jit(solution)/shard_map/psum | solution.py:73
  606.2 0.1 copy.13
  606.2 2.9 cholesky.16
  609.2 0.6 compare_reduce_fusion
  609.8 0.7 fusion.12
  610.5 2.4 custom-call.7
  612.9 0.9 convolution_multiply_fusion
  (43 shorter events, 0.6 us)
Async XLA Ops:
  6.5 519.0 %reduce-scatter.4.cloned.1.call-start = ((), (), s32[]{:S(2)}) async-start(), calls=%async_computation.1 | async-start | bytes 1671168
  206.7 38.6 %copy-start = (bf16[32,192]{1,0:T(8,128)(2,1)S(1)}, bf16[32,192]{1,0:T(8,128)(2,1)}, u32[]{:S(2)}) copy-start(bf16[32,192]{1,0:T(8,128)(2,1)} %param.7) | copy-start | bytes 36868
Sparse Core Ops, SparseCore 0:
  327.3 198.1 reduce-scatter.3
where the time goes:
time: 621 us
  blocking collectives  403 us (65%)
  waiting for transfers between devices  139 us (22%)
  matrix products  36.2 us (6%)
  local copies, waits for them, and re-layouts  19 us (3%)
  between operations  14.6 us (2%)
  other arithmetic  8.63 us (1%)
    unnamed x2, waiting for transfers between devices  139 us
    unnamed x2, blocking collectives  121 us
    psum x1, blocking collectives, on_device(): lax.psum(jnp.dot(image_rows, image_rows.T, precision=lax.Precision.HIGHES...  79.5 us
    psum x1, blocking collectives, on_device(): row_degree = 1.0 + lax.psum(row_sums.reshape(row_count), 'col')  58.9 us
    psum x1, blocking collectives, on_device(): col_degree = 1.0 + lax.psum(col_sums, 'row')  50.4 us
    all_gather x1, blocking collectives, on_device(): lax.all_gather(units_own, 'col', axis=0, tiled=True)  42.2 us
    all_gather x1, blocking collectives, on_device(): lax.all_gather(units_own, 'row', axis=0, tiled=True)  30 us
    dot_general x8, matrix products, weight_tile(): jnp.dot(units_block, col_units.T, preferred_element_type=jnp.float32)  25 us
  transfers between devices with their start and end apart: 1, of which 1 were waited for; matrix products, arithmetic and copies ran while one was open for 0% of the time, Pallas kernels for 0%

commit v1 on v0

v1 whole, which is shorter than its diff:
```python
import math

import jax
import jax.numpy as jnp
from jax import lax
from jax.experimental import pallas as pl
from jax.experimental.pallas import tpu as pltpu
from jax.sharding import PartitionSpec as P

MESH = pl.DeviceIdType.MESH
SEG, E, K = 192, 128, 32
NX, NY, NZ = 4, 4, 8
NPTS = SEG * NX * NY * NZ * 2
SIDE = SEG * 16
UROWS, XROWS, ZROWS = 192, 208, 272
BETA = 2.0 * math.sqrt(E)
SCALE = BETA * math.log2(math.e)
THETA = math.exp(5.0)
PAIR = 2 * SEG
HI = lax.Precision.HIGHEST


def pair_tail(first, second):
    return first + pltpu.roll(second, 64, 1)


def kernel(emb, rec, basis, out, zbuf, xbuf, uc, uo, idc, ido, tile, racc, dpart, dbuf,
           scaled, isend, irecv, gsend, grecv, hsend, hrecv, ssem, rsem):
    r = lax.axis_index("row")
    c = lax.axis_index("col")
    x, y, z, k = r // 4, (c % 2) * 2 + (r // 2) % 2, c // 2, r % 2

    def dev(px, py, pz, pk):
        return (px * 4 + (py % 2) * 2 + pk, pz * 2 + py // 2)

    def zdev(dz, dk):
        return dev(x, y, (z + dz) % NZ, (k + dk) % 2)

    def xydev(dx, dy):
        return dev((x + dx) % NX, (y + dy) % NY, z, k)

    zpeers = [(dz, dk) for dz in (4, 3, 5, 2, 6, 1, 7, 0) for dk in (0, 1) if (dz, dk) != (0, 0)]
    xypeers = [(dx, dy) for dx in (2, 1, 3, 0) for dy in (2, 1, 3, 0) if (dx, dy) != (0, 0)]

    barrier = pltpu.get_barrier_semaphore()
    for p in zpeers:
        pl.semaphore_signal(barrier, inc=1, device_id=zdev(*p), device_id_type=MESH)
    for p in xypeers:
        pl.semaphore_signal(barrier, inc=1, device_id=xydev(*p), device_id_type=MESH)

    values = emb[...].astype(jnp.float32)
    scale = lax.rsqrt(jnp.mean(values * values, axis=1, keepdims=True) + 1e-06) / math.sqrt(E)
    units = (values * scale).astype(jnp.bfloat16)
    ids = rec[...]
    parts = []
    for lanes in (slice(0, 128), slice(128, 192)):
        piece = ids[:, lanes]
        if piece.shape[1] < 128:
            piece = jnp.concatenate([piece, jnp.zeros_like(piece)], axis=1)
        parts += [(piece >> 8).astype(jnp.float32), (piece & 255).astype(jnp.float32)]
    idrows = jnp.concatenate(parts + [jnp.zeros((12, 128), jnp.float32)], axis=0)
    start = basis[...].astype(jnp.float32)
    tail = jnp.concatenate([start[:, 128:192], jnp.zeros((K, 64), jnp.float32)], axis=1)
    message = jnp.concatenate(
        [units, idrows.astype(jnp.bfloat16), start[:, 0:128].astype(jnp.bfloat16), tail.astype(jnp.bfloat16)], axis=0
    )
    own = zbuf.at[k]
    own[...] = message
    xbuf[0] = message[0:XROWS]
    pl.semaphore_wait(barrier, 30)

    sends = []

    def push(src, dst, group, slot, to):
        copy = pltpu.make_async_remote_copy(
            src_ref=src, dst_ref=dst, send_sem=ssem.at[group, slot], recv_sem=rsem.at[group, slot],
            device_id=to, device_id_type=MESH,
        )
        copy.start()
        sends.append(copy)
        return copy

    def zslot(dz, dk):
        return ((NZ - dz) % NZ) * 2 + dk

    def xyslot(dx, dy):
        return ((NX - dx) % NX) * 4 + (NY - dy) % NY

    near = [1, 7, 2, 6, 3, 5, 4]
    direct, handed = {}, {}
    for dz in near:
        d = (NZ - dz) % NZ
        direct[d] = push(own, zbuf.at[2 * d + k], 0, d, zdev(dz, 0))
    handed[0] = push(own, own, 1, 0, zdev(0, 1))
    gathered = []
    for p in sorted(xypeers, key=lambda p: min(p[0], 4 - p[0]) + min(p[1], 4 - p[1])):
        s = xyslot(*p)
        gathered.append(push(zbuf.at[k, 0:XROWS], xbuf.at[s], 2, s, xydev(*p)))
    for d in near:
        direct[d].wait_recv()
        handed[d] = push(zbuf.at[2 * d + k], zbuf.at[2 * d + k], 1, d, zdev(0, 1))
    for d in handed:
        handed[d].wait_recv()
    for copy in gathered:
        copy.wait_recv()

    def lane_ids(buf, s):
        rows = buf[s, UROWS:XROWS].astype(jnp.float32)
        return rows[0:1] * 256.0 + rows[1:2], rows[2:3] * 256.0 + rows[3:4]

    for m in range(8):
        a, b = 2 * m, 2 * m + 1
        for buf, dst in ((zbuf, uc), (xbuf, uo)):
            dst[PAIR * m:PAIR * m + 128] = buf[a, 0:128]
            dst[PAIR * m + 128:PAIR * m + 256] = buf[b, 0:128]
            dst[PAIR * m + 256:PAIR * m + 320] = buf[a, 128:192]
            dst[PAIR * m + 320:PAIR * m + 384] = buf[b, 128:192]
        main_a, tail_a = lane_ids(xbuf, a)
        main_b, tail_b = lane_ids(xbuf, b)
        for t, row in enumerate((main_a, main_b, pair_tail(tail_a, tail_b))):
            ido[0:1, PAIR * m + 128 * t:PAIR * m + 128 * (t + 1)] = row
        main_a, tail_a = lane_ids(zbuf, a)
        main_b, tail_b = lane_ids(zbuf, b)
        for t, row in enumerate((main_a, main_b, pair_tail(tail_a, tail_b))):
            idc[PAIR * m + 128 * t:PAIR * m + 128 * (t + 1), :] = jnp.broadcast_to(row, (128, 128)).T

    racc[...] = jnp.zeros_like(racc)

    def chunk(n, carry):
        start_lane = pl.multiple_of(n * PAIR, PAIR)
        cosine = lax.dot_general(
            uc[...], uo[pl.ds(start_lane, PAIR), :], (((1,), (1,)), ((), ())),
            preferred_element_type=jnp.float32,
        )
        total = racc[...]
        for t in range(3):
            lanes = pl.ds(pl.multiple_of(start_lane + 128 * t, 128), 128)
            weights = jnp.maximum(jnp.exp2(cosine[:, 128 * t:128 * (t + 1)] * SCALE) - THETA, 0.0)
            weights = jnp.where(idc[...] == ido[0:1, lanes], 0.0, weights)
            tile[:, lanes] = weights.astype(jnp.bfloat16)
            total = total + weights
        racc[...] = total
        return carry

    lax.fori_loop(0, 8, chunk, 0)

    for d in range(8):
        place = (z + d) % NZ
        for t in range(3):
            block = racc[PAIR * d + 128 * t:PAIR * d + 128 * (t + 1), :].T
            dpart[pl.ds(place * 3 + t, 1), :] = jnp.sum(block, axis=0, keepdims=True)
    copies = []
    for p in zpeers:
        s = zslot(*p)
        copies.append(push(dpart, dbuf.at[s], 3, s, zdev(*p)))
    degree = dpart[...]
    for copy, p in zip(copies, zpeers):
        copy.wait_recv()
        degree = degree + dbuf[zslot(*p)]
    dbuf[0] = lax.rsqrt(1.0 + degree * (1.0 / THETA))

    for d in range(8):
        place = (z + d) % NZ
        a, b = 2 * d, 2 * d + 1
        pieces = (
            zbuf[a, 208:240].astype(jnp.float32),
            zbuf[b, 208:240].astype(jnp.float32),
            pair_tail(zbuf[a, 240:272].astype(jnp.float32), zbuf[b, 240:272].astype(jnp.float32)),
        )
        for t, piece in enumerate(pieces):
            row = dbuf[0, pl.ds(place * 3 + t, 1), :]
            scaled[:, PAIR * d + 128 * t:PAIR * d + 128 * (t + 1)] = (piece * row).astype(jnp.bfloat16)

    low = lax.broadcasted_iota(jnp.int32, (16, 128), 1) < 64
    copies = []
    for m in (5, 7, 4, 6, 3, 2, 1, 0):
        image = jnp.dot(scaled[...], tile[:, PAIR * m:PAIR * (m + 1)], preferred_element_type=jnp.float32)
        tails = image[:, 256:384]
        turned = pltpu.roll(tails, 64, 1)
        tail_a = jnp.where(low, tails[0:16], turned[16:32])
        tail_b = jnp.where(low, turned[0:16], tails[16:32])
        for s, main, packed in ((2 * m, image[:, 0:128], tail_a), (2 * m + 1, image[:, 128:256], tail_b)):
            isend[s, 0:32] = main.astype(isend.dtype)
            isend[s, 32:48] = packed.astype(isend.dtype)
            if s:
                dx, dy = s // 4, s % 4
                t = xyslot(dx, dy)
                copies.append((t, push(isend.at[s], irecv.at[t], 4, t, xydev(dx, dy))))
            else:
                held = jnp.concatenate([main, packed], axis=0)
    for t, copy in copies:
        copy.wait_recv()
        held = held + irecv[t].astype(jnp.float32)
    low32 = lax.broadcasted_iota(jnp.int32, (K, 128), 1) < 64
    rest = held[32:48]
    rest = jnp.concatenate([rest, pltpu.roll(rest, 64, 1)], axis=0)
    dmain = dbuf[0, pl.ds(z * 3 + k, 1), :]
    dtail = dbuf[0, pl.ds(z * 3 + 2, 1), :]
    dtail = jnp.where(k == 0, dtail, pltpu.roll(dtail, 64, 1))
    img0 = held[0:32] * (dmain * (1.0 / THETA))
    img1 = jnp.where(low32, rest * (dtail * (1.0 / THETA)), 0.0)

    nt = (((1,), (1,)), ((), ()))
    gram = lax.dot_general(img0, img0, nt, precision=HI, preferred_element_type=jnp.float32)
    gram = gram + lax.dot_general(img1, img1, nt, precision=HI, preferred_element_type=jnp.float32)
    gram = jnp.concatenate([gram[8 * g:8 * g + 8] for g in range(4)], axis=1)
    gsend[...] = gram
    copies = []
    for p in xypeers:
        s = xyslot(*p)
        copies.append((s, push(gsend, grecv.at[s], 5, s, xydev(*p))))
    for s, copy in copies:
        copy.wait_recv()
        gram = gram + grecv[s]
    hsend[...] = gram
    copies = []
    for p in zpeers:
        s = zslot(*p)
        copies.append((s, push(hsend, hrecv.at[s], 6, s, zdev(*p))))
    hrecv[0] = gram
    for s, copy in copies:
        copy.wait_recv()
    for s, copy in copies:
        gram = gram + hrecv[s]
    gram = jnp.concatenate([gram] + [pltpu.roll(gram, 128 - 32 * g, 1) for g in range(1, 4)], axis=0)

    lane = lax.broadcasted_iota(jnp.int32, (K, 128), 1)
    sub = lax.broadcasted_iota(jnp.int32, (K, 128), 0)
    side = jnp.where(lane < 64, img1, pltpu.roll(jnp.where(lane < 32, gram, 0.0), 64, 1))
    for j in range(K - 1):
        pivot = side[j:j + 1, 64 + j:65 + j]
        factor = jnp.where(sub > j, side[:, 64 + j:65 + j] * (1.0 / pivot), 0.0)
        img0 = img0 - factor * img0[j:j + 1]
        side = side - factor * side[j:j + 1]
    diag = jnp.sum(jnp.where(lane == sub + 64, side, 0.0), axis=1, keepdims=True)
    final = lax.rsqrt(diag) * math.sqrt(NPTS)
    out[:, 0:128] = img0 * final
    out[:, 128:192] = (side * final)[:, 0:64]
    for copy in sends:
        copy.wait_send()


def on_device(embeddings, recordings, start_basis):
    f32, bf16 = jnp.float32, jnp.bfloat16
    return pl.pallas_call(
        kernel,
        out_shape=jax.ShapeDtypeStruct((K, SEG), f32),
        in_specs=[pl.BlockSpec(memory_space=pltpu.VMEM)] * 3,
        out_specs=pl.BlockSpec(memory_space=pltpu.VMEM),
        scratch_shapes=[
            pltpu.VMEM((16, ZROWS, 128), bf16),
            pltpu.VMEM((16, XROWS, 128), bf16),
            pltpu.VMEM((SIDE, 128), bf16),
            pltpu.VMEM((SIDE, 128), bf16),
            pltpu.VMEM((SIDE, 128), f32),
            pltpu.VMEM((8, SIDE), f32),
            pltpu.VMEM((SIDE, SIDE), bf16),
            pltpu.VMEM((SIDE, 128), f32),
            pltpu.VMEM((24, 128), f32),
            pltpu.VMEM((16, 24, 128), f32),
            pltpu.VMEM((K, SIDE), bf16),
            pltpu.VMEM((16, 48, 128), bf16),
            pltpu.VMEM((16, 48, 128), bf16),
            pltpu.VMEM((8, 128), f32),
            pltpu.VMEM((16, 8, 128), f32),
            pltpu.VMEM((8, 128), f32),
            pltpu.VMEM((16, 8, 128), f32),
            pltpu.SemaphoreType.DMA((7, 16)),
            pltpu.SemaphoreType.DMA((7, 16)),
        ],
        compiler_params=pltpu.CompilerParams(
            collective_id=0, has_side_effects=True, vmem_limit_bytes=56 * 2**20
        ),
    )(embeddings, recordings.reshape(1, SEG), start_basis)


def solution(mesh):
    in_specs = (P(("row", "col"), None), P(("row", "col")), P(None, ("row", "col")))
    out_specs = P(None, ("row", "col"))
    return jax.shard_map(
        on_device, mesh=mesh, in_specs=in_specs, out_specs=out_specs, check_vma=False
    )
```

time: 621 us -> 74.2 us (0.12)
  blocking collectives: 403 us -> 0 us
  waiting for transfers between devices: 139 us -> 0 us
  Pallas kernels: 0 us -> 72.6 us
  matrix products: 36.2 us -> 0 us
  local copies, waits for them, and re-layouts: 19 us -> 1.38 us
  between operations: 14.6 us -> 0.01 us
  other arithmetic: 8.63 us -> 0 us
    psum x3 -> x0, blocking collectives: 189 us -> none  [the longest x1 79.5 us: on_device(): lax.psum(jnp.dot(image_rows, image_rows.T, precision=lax.Precision.HIGHES...]
    unnamed x2 -> x0, waiting for transfers between devices: 139 us -> none
    unnamed x2 -> x0, blocking collectives: 121 us -> none
    all_gather x3 -> x0, blocking collectives: 93.1 us -> none  [the longest x1 42.2 us: on_device(): lax.all_gather(units_own, 'col', axis=0, tiled=True)]
    pallas_call x0 -> x1, Pallas kernels: none -> 72.6 us  [on_device(): pl.pallas_call(kernel, out_shape=jax.ShapeDtypeStruct((K, SEG), f32), in_...]
    dot_general x9 -> x0, matrix products: 25.2 us -> none  [the longest x8 25 us: weight_tile(): jnp.dot(units_block, col_units.T, preferred_element_type=jnp.float32)]
    dynamic_update_slice x16 -> x0, local copies, waits for them, and re-layouts: 13.1 us -> none  [on_device(): lax.scan(first_pass, jnp.zeros((col_count,), jnp.float32), (unit_blocks,...]
    unnamed x1 -> x0, matrix products: 10.1 us -> none
  transfers between devices with their start and end apart: 1 -> 0, of which waited for: 1 -> 0; matrix products, arithmetic and copies ran while one was open for 0% -> 0% of each run, Pallas kernels for 0% -> 0%
where the time goes in v1:
time: 74.2 us; the launch traced here: 74 us
  Pallas kernels  72.6 us (98%)
  local copies, waits for them, and re-layouts  1.38 us (2%)
    pallas_call x1, Pallas kernels, on_device(): pl.pallas_call(kernel, out_shape=jax.ShapeDtypeStruct((K, SEG), f32), in_...  72.6 us

profile of v1, /device:TPU:1, one launch (start us, length us, event | category | flops | bytes accessed | tf_op | source)
XLA Modules:
  0.0 74.0 jit_solution(8429144675221702649)
XLA Ops:
  0.0 72.6 %shard_map.37 = f32[32,192]{1,0:T(8,128)} custom-call(bf16[192,128]{1,0:T(8,128)(2,1)} %emb.1, s32[1,192]{1,0:T(1,128)} %bitcast.1, bf16[32,192]{1,0:T(8,128)(2,1)} %basis.1), custom_call_target="tpu_custom_call" | custom-call | tf_op jit(solution)/shard_map/pallas_call | solution.py:245
  72.6 1.4 %copy.5 = f32[32,192]{1,0:T(8,128)} copy(f32[32,192]{1,0:T(8,128)} %shard_map.37) | data formatting | bytes 49152

commit v2 on v1

--- a/solution.py
+++ b/solution.py
@@ -12,7 +12,12 @@
 NX, NY, NZ = 4, 4, 8
 NPTS = SEG * NX * NY * NZ * 2
 SIDE = SEG * 16
-UROWS, XROWS, ZROWS = 192, 208, 272
+UROWS, XROWS = 192, 208
+ZORDER = (0, 7, 1, 6, 2, 5, 3, 4)
+XORDER = (
+    (0, 0), (3, 0), (1, 0), (0, 3), (0, 1), (2, 0), (3, 3), (3, 1),
+    (1, 3), (1, 1), (0, 2), (3, 2), (1, 2), (2, 3), (2, 1), (2, 2),
+)
 BETA = 2.0 * math.sqrt(E)
 SCALE = BETA * math.log2(math.e)
 THETA = math.exp(5.0)
@@ -24,7 +29,7 @@
     return first + pltpu.roll(second, 64, 1)
 
 
-def kernel(emb, rec, basis, out, zbuf, xbuf, uc, uo, idc, ido, tile, racc, dpart, dbuf,
+def kernel(emb, rec, basis, out, zbuf, xbuf, bbuf, uc, uo, idc, ido, tile, racc, dpart, dbuf,
            scaled, isend, irecv, gsend, grecv, hsend, hrecv, ssem, rsem):
     r = lax.axis_index("row")
     c = lax.axis_index("col")
@@ -36,8 +41,11 @@
     def zdev(dz, dk):
         return dev(x, y, (z + dz) % NZ, (k + dk) % 2)
 
-    def xydev(dx, dy):
-        return dev((x + dx) % NX, (y + dy) % NY, z, k)
+    lead = k == 0
+
+    def xydev(da, db):
+        dx, dy = jnp.where(lead, da, db), jnp.where(lead, db, da)
+        return dev((x + dx + NX) % NX, (y + dy + NY) % NY, z, k)
 
     zpeers = [(dz, dk) for dz in (4, 3, 5, 2, 6, 1, 7, 0) for dk in (0, 1) if (dz, dk) != (0, 0)]
     xypeers = [(dx, dy) for dx in (2, 1, 3, 0) for dy in (2, 1, 3, 0) if (dx, dy) != (0, 0)]
@@ -61,15 +69,14 @@
     idrows = jnp.concatenate(parts + [jnp.zeros((12, 128), jnp.float32)], axis=0)
     start = basis[...].astype(jnp.float32)
     tail = jnp.concatenate([start[:, 128:192], jnp.zeros((K, 64), jnp.float32)], axis=1)
-    message = jnp.concatenate(
-        [units, idrows.astype(jnp.bfloat16), start[:, 0:128].astype(jnp.bfloat16), tail.astype(jnp.bfloat16)], axis=0
-    )
     own = zbuf.at[k]
-    own[...] = message
-    xbuf[0] = message[0:XROWS]
+    own[...] = jnp.concatenate([units, idrows.astype(jnp.bfloat16)], axis=0)
+    bown = bbuf.at[k]
+    bown[...] = jnp.concatenate([start[:, 0:128], tail], axis=0).astype(jnp.bfloat16)
+
+    racc[...] = jnp.zeros_like(racc)
+    sends = []
     pl.semaphore_wait(barrier, 30)
-
-    sends = []
 
     def push(src, dst, group, slot, to):
         copy = pltpu.make_async_remote_copy(
@@ -86,68 +93,144 @@
     def xyslot(dx, dy):
         return ((NX - dx) % NX) * 4 + (NY - dy) % NY
 
-    near = [1, 7, 2, 6, 3, 5, 4]
-    direct, handed = {}, {}
-    for dz in near:
-        d = (NZ - dz) % NZ
-        direct[d] = push(own, zbuf.at[2 * d + k], 0, d, zdev(dz, 0))
-    handed[0] = push(own, own, 1, 0, zdev(0, 1))
-    gathered = []
-    for p in sorted(xypeers, key=lambda p: min(p[0], 4 - p[0]) + min(p[1], 4 - p[1])):
-        s = xyslot(*p)
-        gathered.append(push(zbuf.at[k, 0:XROWS], xbuf.at[s], 2, s, xydev(*p)))
-    for d in near:
-        direct[d].wait_recv()
-        handed[d] = push(zbuf.at[2 * d + k], zbuf.at[2 * d + k], 1, d, zdev(0, 1))
-    for d in handed:
-        handed[d].wait_recv()
-    for copy in gathered:
-        copy.wait_recv()
+    hop, relayed, plane = {}, {}, {}
+
+    def zblock(d):
+        return zbuf.at[2 * (d % NZ) + k]
+
+    def zhop(d, step):
+        t = (d - step) % NZ
+        hop[t] = push(zblock(d), zblock(t), 0, t, zdev(step, 0))
+
+    def relay(d):
+        relayed[d] = push(zblock(d), zblock(d), 1, d, zdev(0, 1))
+
+    def pblock(da, db):
+        return own if (da, db) == (0, 0) else xbuf.at[da * 4 + db]
+
+    def phop(da, db, sa, sb):
+        t = ((da - sa) % 4, (db - sb) % 4)
+        plane[t] = push(pblock(da, db), xbuf.at[t[0] * 4 + t[1]], 2, t[0] * 4 + t[1], xydev(sa, sb))
+
+    zhop(0, 2)
+    zhop(0, -2)
+    phop(0, 0, 1, 0)
+    phop(0, 0, -1, 0)
+    zhop(0, 1)
+    zhop(0, -1)
+    relay(0)
+    phop(0, 0, 0, 1)
+    phop(0, 0, 0, -1)
+    phop(0, 0, 2, 0)
+    plane[3, 0].wait_recv()
+    for step in (1, -1, 2):
+        phop(3, 0, 0, step)
+    plane[1, 0].wait_recv()
+    for step in (1, -1, 2):
+        phop(1, 0, 0, step)
+    hop[6].wait_recv()
+    zhop(6, 1)
+    hop[2].wait_recv()
+    zhop(2, -1)
+    turn = jnp.where(lead, 6, 2)
+    hop[4] = push(zblock(turn), zblock(4), 0, 4, zdev(jnp.where(lead, 2, NZ - 2), 0))
+    relay(6)
+    relay(2)
+    hop[7].wait_recv()
+    relay(7)
+    hop[1].wait_recv()
+    relay(1)
+    plane[0, 1].wait_recv()
+    phop(0, 1, 0, -1)
+    plane[2, 0].wait_recv()
+    for step in (1, -1, 2):
+        phop(2, 0, 0, step)
+    plane[0, 3].wait_recv()
 
     def lane_ids(buf, s):
         rows = buf[s, UROWS:XROWS].astype(jnp.float32)
         return rows[0:1] * 256.0 + rows[1:2], rows[2:3] * 256.0 + rows[3:4]
 
-    for m in range(8):
-        a, b = 2 * m, 2 * m + 1
-        for buf, dst in ((zbuf, uc), (xbuf, uo)):
-            dst[PAIR * m:PAIR * m + 128] = buf[a, 0:128]
-            dst[PAIR * m + 128:PAIR * m + 256] = buf[b, 0:128]
-            dst[PAIR * m + 256:PAIR * m + 320] = buf[a, 128:192]
-            dst[PAIR * m + 320:PAIR * m + 384] = buf[b, 128:192]
-        main_a, tail_a = lane_ids(xbuf, a)
-        main_b, tail_b = lane_ids(xbuf, b)
-        for t, row in enumerate((main_a, main_b, pair_tail(tail_a, tail_b))):
-            ido[0:1, PAIR * m + 128 * t:PAIR * m + 128 * (t + 1)] = row
-        main_a, tail_a = lane_ids(zbuf, a)
-        main_b, tail_b = lane_ids(zbuf, b)
-        for t, row in enumerate((main_a, main_b, pair_tail(tail_a, tail_b))):
-            idc[PAIR * m + 128 * t:PAIR * m + 128 * (t + 1), :] = jnp.broadcast_to(row, (128, 128)).T
-
-    racc[...] = jnp.zeros_like(racc)
-
-    def chunk(n, carry):
-        start_lane = pl.multiple_of(n * PAIR, PAIR)
+    def repack(buf, a, b, dst, m):
+        dst[PAIR * m:PAIR * m + 128] = buf[a, 0:128]
+        dst[PAIR * m + 128:PAIR * m + 256] = buf[b, 0:128]
+        dst[PAIR * m + 256:PAIR * m + 320] = buf[a, 128:192]
+        dst[PAIR * m + 320:PAIR * m + 384] = buf[b, 128:192]
+        main_a, tail_a = lane_ids(buf, a)
+        main_b, tail_b = lane_ids(buf, b)
+        return [(PAIR * m + 128 * t, row) for t, row in enumerate((main_a, main_b, pair_tail(tail_a, tail_b)))]
+
+    def take_z(m):
+        d = ZORDER[m]
+        relayed[d].wait_recv()
+        for at, row in repack(zbuf, 2 * d, 2 * d + 1, uc, m):
+            idc[at:at + 128, :] = jnp.broadcast_to(row, (128, 128)).T
+
+    def take_xy(m):
+        first, second = XORDER[2 * m], XORDER[2 * m + 1]
+        for at, row in repack(xbuf, first[0] * 4 + first[1], second[0] * 4 + second[1], uo, m):
+            ido[0:1, at:at + 128] = row
+
+    def affinity(rows, n):
+        lane0 = pl.multiple_of(2 * PAIR * n, 2 * PAIR)
         cosine = lax.dot_general(
-            uc[...], uo[pl.ds(start_lane, PAIR), :], (((1,), (1,)), ((), ())),
+            uc[rows, :], uo[pl.ds(lane0, 2 * PAIR), :], (((1,), (1,)), ((), ())),
             preferred_element_type=jnp.float32,
         )
-        total = racc[...]
-        for t in range(3):
-            lanes = pl.ds(pl.multiple_of(start_lane + 128 * t, 128), 128)
+        total = racc[rows, :]
+        for t in range(6):
+            lanes = pl.ds(pl.multiple_of(lane0 + 128 * t, 128), 128)
             weights = jnp.maximum(jnp.exp2(cosine[:, 128 * t:128 * (t + 1)] * SCALE) - THETA, 0.0)
-            weights = jnp.where(idc[...] == ido[0:1, lanes], 0.0, weights)
-            tile[:, lanes] = weights.astype(jnp.bfloat16)
+            weights = jnp.where(idc[rows, :] == ido[0:1, lanes], 0.0, weights)
+            tile[rows, lanes] = weights.astype(jnp.bfloat16)
             total = total + weights
-        racc[...] = total
-        return carry
-
-    lax.fori_loop(0, 8, chunk, 0)
-
-    for d in range(8):
+        racc[rows, :] = total
+
+    def two(rows, n):
+        def body(i, carry):
+            affinity(rows, n + i)
+            return carry
+
+        lax.fori_loop(0, 2, body, 0)
+
+    near, far = slice(0, 5 * PAIR), slice(5 * PAIR, 8 * PAIR)
+    xbuf[0] = own[...]
+    for m in range(2):
+        take_xy(m)
+    for m in range(5):
+        take_z(m)
+    affinity(near, 0)
+    for d in (5, 3, 4):
+        hop[d].wait_recv()
+        relay(d)
+    bases = []
+    for dz, dk in zpeers:
+        s = zslot(dz, dk)
+        bases.append(push(bown, bbuf.at[2 * (s // 2) + k], 7, s, zdev(dz, dk)))
+    for s in ((3, 3), (3, 1)):
+        plane[s].wait_recv()
+    for m in (2, 3):
+        take_xy(m)
+    affinity(near, 1)
+    for m in (5, 6, 7):
+        take_z(m)
+    two(far, 0)
+    for s in ((1, 3), (1, 1), (0, 2), (3, 2)):
+        plane[s].wait_recv()
+    for m in (4, 5):
+        take_xy(m)
+    affinity(near, 2)
+    for s in ((1, 2), (2, 3), (2, 1), (2, 2)):
+        plane[s].wait_recv()
+    for m in (6, 7):
+        take_xy(m)
+    affinity(near, 3)
+    two(far, 2)
+
+    for m, d in enumerate(ZORDER):
         place = (z + d) % NZ
         for t in range(3):
-            block = racc[PAIR * d + 128 * t:PAIR * d + 128 * (t + 1), :].T
+            block = racc[PAIR * m + 128 * t:PAIR * m + 128 * (t + 1), :].T
             dpart[pl.ds(place * 3 + t, 1), :] = jnp.sum(block, axis=0, keepdims=True)
     copies = []
     for p in zpeers:
@@ -159,33 +242,31 @@
         degree = degree + dbuf[zslot(*p)]
     dbuf[0] = lax.rsqrt(1.0 + degree * (1.0 / THETA))
 
-    for d in range(8):
+    for copy in bases:
+        copy.wait_recv()
+    for m, d in enumerate(ZORDER):
         place = (z + d) % NZ
-        a, b = 2 * d, 2 * d + 1
-        pieces = (
-            zbuf[a, 208:240].astype(jnp.float32),
-            zbuf[b, 208:240].astype(jnp.float32),
-            pair_tail(zbuf[a, 240:272].astype(jnp.float32), zbuf[b, 240:272].astype(jnp.float32)),
-        )
+        a, b = bbuf[2 * d].astype(jnp.float32), bbuf[2 * d + 1].astype(jnp.float32)
+        pieces = (a[0:K], b[0:K], pair_tail(a[K:2 * K], b[K:2 * K]))
         for t, piece in enumerate(pieces):
             row = dbuf[0, pl.ds(place * 3 + t, 1), :]
-            scaled[:, PAIR * d + 128 * t:PAIR * d + 128 * (t + 1)] = (piece * row).astype(jnp.bfloat16)
+            scaled[:, PAIR * m + 128 * t:PAIR * m + 128 * (t + 1)] = (piece * row).astype(jnp.bfloat16)
 
     low = lax.broadcasted_iota(jnp.int32, (16, 128), 1) < 64
     copies = []
-    for m in (5, 7, 4, 6, 3, 2, 1, 0):
+    for m in range(7, -1, -1):
         image = jnp.dot(scaled[...], tile[:, PAIR * m:PAIR * (m + 1)], preferred_element_type=jnp.float32)
         tails = image[:, 256:384]
         turned = pltpu.roll(tails, 64, 1)
         tail_a = jnp.where(low, tails[0:16], turned[16:32])
         tail_b = jnp.where(low, turned[0:16], tails[16:32])
-        for s, main, packed in ((2 * m, image[:, 0:128], tail_a), (2 * m + 1, image[:, 128:256], tail_b)):
+        for (da, db), main, packed in ((XORDER[2 * m], image[:, 0:128], tail_a), (XORDER[2 * m + 1], image[:, 128:256], tail_b)):
+            s = da * 4 + db
             isend[s, 0:32] = main.astype(isend.dtype)
             isend[s, 32:48] = packed.astype(isend.dtype)
             if s:
-                dx, dy = s // 4, s % 4
-                t = xyslot(dx, dy)
-                copies.append((t, push(isend.at[s], irecv.at[t], 4, t, xydev(dx, dy))))
+                t = xyslot(da, db)
+                copies.append((t, push(isend.at[s], irecv.at[t], 4, t, xydev(da, db))))
             else:
                 held = jnp.concatenate([main, packed], axis=0)
     for t, copy in copies:
@@ -217,7 +298,6 @@
     for p in zpeers:
         s = zslot(*p)
         copies.append((s, push(hsend, hrecv.at[s], 6, s, zdev(*p))))
-    hrecv[0] = gram
     for s, copy in copies:
         copy.wait_recv()
     for s, copy in copies:
@@ -248,8 +328,9 @@
         in_specs=[pl.BlockSpec(memory_space=pltpu.VMEM)] * 3,
         out_specs=pl.BlockSpec(memory_space=pltpu.VMEM),
         scratch_shapes=[
-            pltpu.VMEM((16, ZROWS, 128), bf16),
             pltpu.VMEM((16, XROWS, 128), bf16),
+            pltpu.VMEM((16, XROWS, 128), bf16),
+            pltpu.VMEM((16, 2 * K, 128), bf16),
             pltpu.VMEM((SIDE, 128), bf16),
             pltpu.VMEM((SIDE, 128), bf16),
             pltpu.VMEM((SIDE, 128), f32),
@@ -265,11 +346,11 @@
             pltpu.VMEM((16, 8, 128), f32),
             pltpu.VMEM((8, 128), f32),
             pltpu.VMEM((16, 8, 128), f32),
-            pltpu.SemaphoreType.DMA((7, 16)),
-            pltpu.SemaphoreType.DMA((7, 16)),
+            pltpu.SemaphoreType.DMA((8, 16)),
+            pltpu.SemaphoreType.DMA((8, 16)),
         ],
         compiler_params=pltpu.CompilerParams(
-            collective_id=0, has_side_effects=True, vmem_limit_bytes=56 * 2**20
+            collective_id=0, has_side_effects=True, vmem_limit_bytes=60 * 2**20
         ),
     )(embeddings, recordings.reshape(1, SEG), start_basis)
 

time: 74.2 us -> 65.4 us (0.88)
  Pallas kernels: 72.6 us -> 63.9 us
    pallas_call x1, Pallas kernels: 72.6 us -> 63.9 us  [on_device(): pl.pallas_call(kernel, out_shape=jax.ShapeDtypeStruct((K, SEG), f32), in_...]
where the time goes in v2:
time: 65.4 us; the launch traced here: 65.2 us
  Pallas kernels  63.9 us (98%)
  local copies, waits for them, and re-layouts  1.38 us (2%)
    pallas_call x1, Pallas kernels, on_device(): pl.pallas_call(kernel, out_shape=jax.ShapeDtypeStruct((K, SEG), f32), in_...  63.9 us
    unnamed x1, local copies, waits for them, and re-layouts  1.38 us

profile of v2, /device:TPU:1, one launch (start us, length us, event | category | flops | bytes accessed | tf_op | source)
XLA Modules:
  0.0 65.2 jit_solution(12635364401079977513)
XLA Ops:
  0.0 63.9 %shard_map.37 = f32[32,192]{1,0:T(8,128)} custom-call(bf16[192,128]{1,0:T(8,128)(2,1)} %emb.1, s32[1,192]{1,0:T(1,128)} %bitcast.1, bf16[32,192]{1,0:T(8,128)(2,1)} %basis.1), custom_call_target="tpu_custom_call" | custom-call | tf_op jit(solution)/shard_map/pallas_call | solution.py:325
  63.9 1.4 %copy.5 = f32[32,192]{1,0:T(8,128)} copy(f32[32,192]{1,0:T(8,128)} %shard_map.37) | data formatting | bytes 49152

commit v3 on v2

--- a/solution.py
+++ b/solution.py
@@ -51,9 +51,9 @@
     xypeers = [(dx, dy) for dx in (2, 1, 3, 0) for dy in (2, 1, 3, 0) if (dx, dy) != (0, 0)]
 
     barrier = pltpu.get_barrier_semaphore()
-    for p in zpeers:
+    for p in ((2, 0), (6, 0), (1, 0), (7, 0), (0, 1)):
         pl.semaphore_signal(barrier, inc=1, device_id=zdev(*p), device_id_type=MESH)
-    for p in xypeers:
+    for p in ((2, 0), (0, 2), (1, 0), (3, 0), (0, 1), (0, 3)):
         pl.semaphore_signal(barrier, inc=1, device_id=xydev(*p), device_id_type=MESH)
 
     values = emb[...].astype(jnp.float32)
@@ -76,7 +76,7 @@
 
     racc[...] = jnp.zeros_like(racc)
     sends = []
-    pl.semaphore_wait(barrier, 30)
+    pl.semaphore_wait(barrier, 11)
 
     def push(src, dst, group, slot, to):
         copy = pltpu.make_async_remote_copy(
@@ -145,7 +145,7 @@
     plane[2, 0].wait_recv()
     for step in (1, -1, 2):
         phop(2, 0, 0, step)
-    plane[0, 3].wait_recv()
+    seen = {(0, 0), (3, 0), (1, 0), (0, 1), (2, 0)}
 
     def lane_ids(buf, s):
         rows = buf[s, UROWS:XROWS].astype(jnp.float32)
@@ -186,46 +186,45 @@
             total = total + weights
         racc[rows, :] = total
 
-    def two(rows, n):
-        def body(i, carry):
-            affinity(rows, n + i)
-            return carry
-
-        lax.fori_loop(0, 2, body, 0)
-
+    first, second = slice(0, 3 * PAIR), slice(3 * PAIR, 5 * PAIR)
     near, far = slice(0, 5 * PAIR), slice(5 * PAIR, 8 * PAIR)
+
+    def take_plane(n):
+        for s in XORDER[4 * n:4 * n + 4]:
+            if s not in seen:
+                plane[s].wait_recv()
+        take_xy(2 * n)
+        take_xy(2 * n + 1)
+
     xbuf[0] = own[...]
-    for m in range(2):
-        take_xy(m)
-    for m in range(5):
+    take_plane(0)
+    for m in range(3):
         take_z(m)
-    affinity(near, 0)
+    affinity(first, 0)
+    for m in (3, 4):
+        take_z(m)
+    affinity(second, 0)
+    take_plane(1)
+    affinity(near, 1)
+    take_plane(2)
+    affinity(near, 2)
     for d in (5, 3, 4):
         hop[d].wait_recv()
         relay(d)
+    take_plane(3)
+    affinity(near, 3)
+    for m in (5, 6, 7):
+        take_z(m)
     bases = []
     for dz, dk in zpeers:
         s = zslot(dz, dk)
         bases.append(push(bown, bbuf.at[2 * (s // 2) + k], 7, s, zdev(dz, dk)))
-    for s in ((3, 3), (3, 1)):
-        plane[s].wait_recv()
-    for m in (2, 3):
-        take_xy(m)
-    affinity(near, 1)
-    for m in (5, 6, 7):
-        take_z(m)
-    two(far, 0)
-    for s in ((1, 3), (1, 1), (0, 2), (3, 2)):
-        plane[s].wait_recv()
-    for m in (4, 5):
-        take_xy(m)
-    affinity(near, 2)
-    for s in ((1, 2), (2, 3), (2, 1), (2, 2)):
-        plane[s].wait_recv()
-    for m in (6, 7):
-        take_xy(m)
-    affinity(near, 3)
-    two(far, 2)
+
+    def body(n, carry):
+        affinity(far, n)
+        return carry
+
+    lax.fori_loop(0, 4, body, 0)
 
     for m, d in enumerate(ZORDER):
         place = (z + d) % NZ

time: 65.4 us -> 64.5 us (0.986)
  Pallas kernels: 63.9 us -> 63 us
    pallas_call x1, Pallas kernels: 63.9 us -> 63 us  [on_device(): pl.pallas_call(kernel, out_shape=jax.ShapeDtypeStruct((K, SEG), f32), in_...]
where the time goes in v3:
time: 64.5 us; the launch traced here: 64.3 us
  Pallas kernels  63 us (98%)
  local copies, waits for them, and re-layouts  1.38 us (2%)
    pallas_call x1, Pallas kernels, on_device(): pl.pallas_call(kernel, out_shape=jax.ShapeDtypeStruct((K, SEG), f32), in_...  63 us
    unnamed x1, local copies, waits for them, and re-layouts  1.38 us

profile of v3, /device:TPU:1, one launch (start us, length us, event | category | flops | bytes accessed | tf_op | source)
XLA Modules:
  0.0 64.3 jit_solution(16090791177222044142)
XLA Ops:
  0.0 63.0 %shard_map.37 = f32[32,192]{1,0:T(8,128)} custom-call(bf16[192,128]{1,0:T(8,128)(2,1)} %emb.1, s32[1,192]{1,0:T(1,128)} %bitcast.1, bf16[32,192]{1,0:T(8,128)(2,1)} %basis.1), custom_call_target="tpu_custom_call" | custom-call | tf_op jit(solution)/shard_map/pallas_call | solution.py:324
  63.0 1.4 %copy.5 = f32[32,192]{1,0:T(8,128)} copy(f32[32,192]{1,0:T(8,128)} %shard_map.37) | data formatting | bytes 49152

commit v4 on v3

--- a/solution.py
+++ b/solution.py
@@ -29,8 +29,8 @@
     return first + pltpu.roll(second, 64, 1)
 
 
-def kernel(emb, rec, basis, out, zbuf, xbuf, bbuf, uc, uo, idc, ido, tile, racc, dpart, dbuf,
-           scaled, isend, irecv, gsend, grecv, hsend, hrecv, ssem, rsem):
+def kernel(emb_hbm, rec_hbm, basis_hbm, out, emb, rec, basis, zbuf, xbuf, bbuf, uc, uo, idc, ido, tile, racc, dnear, dfar, nbuf, fbuf, dinv,
+           scaled, isend, irecv, gsend, grecv, hsend, hrecv, ssem, rsem, isem):
     r = lax.axis_index("row")
     c = lax.axis_index("col")
     x, y, z, k = r // 4, (c % 2) * 2 + (r // 2) % 2, c // 2, r % 2
@@ -55,6 +55,16 @@
         pl.semaphore_signal(barrier, inc=1, device_id=zdev(*p), device_id_type=MESH)
     for p in ((2, 0), (0, 2), (1, 0), (3, 0), (0, 1), (0, 3)):
         pl.semaphore_signal(barrier, inc=1, device_id=xydev(*p), device_id_type=MESH)
+
+    loads = [
+        pltpu.make_async_copy(src, dst, isem.at[i])
+        for i, (src, dst) in enumerate(((emb_hbm, emb), (rec_hbm, rec), (basis_hbm, basis)))
+    ]
+    for load in loads:
+        load.start()
+    racc[...] = jnp.zeros_like(racc)
+    for load in loads:
+        load.wait()
 
     values = emb[...].astype(jnp.float32)
     scale = lax.rsqrt(jnp.mean(values * values, axis=1, keepdims=True) + 1e-06) / math.sqrt(E)
@@ -74,7 +84,6 @@
     bown = bbuf.at[k]
     bown[...] = jnp.concatenate([start[:, 0:128], tail], axis=0).astype(jnp.bfloat16)
 
-    racc[...] = jnp.zeros_like(racc)
     sends = []
     pl.semaphore_wait(barrier, 11)
 
@@ -145,6 +154,19 @@
     plane[2, 0].wait_recv()
     for step in (1, -1, 2):
         phop(2, 0, 0, step)
+    bases, handed = {}, {}
+
+    def basis_to(dz):
+        d = (NZ - dz) % NZ
+        bases[d] = push(bown, bbuf.at[2 * d + k], 7, d, zdev(dz, 0))
+
+    def basis_relay(d):
+        if d:
+            bases[d].wait_recv()
+        handed[d] = push(bbuf.at[2 * d + k], bbuf.at[2 * d + k], 7, 8 + d, zdev(0, 1))
+
+    for dz in (6, 2, 7, 1):
+        basis_to(dz)
     seen = {(0, 0), (3, 0), (1, 0), (0, 1), (2, 0)}
 
     def lane_ids(buf, s):
@@ -177,14 +199,17 @@
             uc[rows, :], uo[pl.ds(lane0, 2 * PAIR), :], (((1,), (1,)), ((), ())),
             preferred_element_type=jnp.float32,
         )
-        total = racc[rows, :]
-        for t in range(6):
-            lanes = pl.ds(pl.multiple_of(lane0 + 128 * t, 128), 128)
-            weights = jnp.maximum(jnp.exp2(cosine[:, 128 * t:128 * (t + 1)] * SCALE) - THETA, 0.0)
-            weights = jnp.where(idc[rows, :] == ido[0:1, lanes], 0.0, weights)
-            tile[rows, lanes] = weights.astype(jnp.bfloat16)
-            total = total + weights
-        racc[rows, :] = total
+        for at in range(rows.start, rows.stop, 16):
+            part = slice(at, at + 16)
+            total = racc[part, :]
+            for t in range(6):
+                lanes = pl.ds(pl.multiple_of(lane0 + 128 * t, 128), 128)
+                piece = cosine[at - rows.start:at - rows.start + 16, 128 * t:128 * (t + 1)]
+                weights = jnp.maximum(jnp.exp2(piece * SCALE) - THETA, 0.0)
+                weights = jnp.where(idc[part, :] == ido[0:1, lanes], 0.0, weights)
+                tile[part, lanes] = weights.astype(jnp.bfloat16)
+                total = total + weights
+            racc[part, :] = total
 
     first, second = slice(0, 3 * PAIR), slice(3 * PAIR, 5 * PAIR)
     near, far = slice(0, 5 * PAIR), slice(5 * PAIR, 8 * PAIR)
@@ -211,14 +236,27 @@
     for d in (5, 3, 4):
         hop[d].wait_recv()
         relay(d)
+    for dz in (4, 3, 5):
+        basis_to(dz)
+    for d in (0, 7, 1, 6, 2):
+        basis_relay(d)
     take_plane(3)
     affinity(near, 3)
     for m in (5, 6, 7):
         take_z(m)
-    bases = []
-    for dz, dk in zpeers:
-        s = zslot(dz, dk)
-        bases.append(push(bown, bbuf.at[2 * (s // 2) + k], 7, s, zdev(dz, dk)))
+
+    def row_sums(ms):
+        sums = {}
+        for m in ms:
+            for t in range(3):
+                block = racc[PAIR * m + 128 * t:PAIR * m + 128 * (t + 1), :].T
+                sums[3 * ((ZORDER[m] + 2) % NZ) + t] = jnp.sum(block, axis=0, keepdims=True)
+        return sums
+
+    for row, value in row_sums(range(5)).items():
+        dnear[row:row + 1, :] = value
+    dnear[15:16, :] = jnp.zeros((1, 128), jnp.float32)
+    near_copies = {p: push(dnear, nbuf.at[zslot(*p)], 3, zslot(*p), zdev(*p)) for p in zpeers}
 
     def body(n, carry):
         affinity(far, n)
@@ -226,29 +264,35 @@
 
     lax.fori_loop(0, 4, body, 0)
 
+    sums = row_sums(range(5, 8))
+    rest = jnp.concatenate([sums[row] for row in range(15, 24)] + [jnp.zeros((7, 128), jnp.float32)], axis=0)
+    dfar[...] = rest.astype(jnp.bfloat16)
+    far_copies = {p: push(dfar, fbuf.at[zslot(*p)], 8, zslot(*p), zdev(*p)) for p in zpeers}
+    for d in (5, 3, 4):
+        basis_relay(d)
+    degree = jnp.concatenate([dnear[0:15], rest[0:9]], axis=0)
+    for dz in (0, 1, 7, 2, 6, 3, 5, 4):
+        part = None
+        for dk in ((1,) if dz == 0 else (0, 1)):
+            near_copies[dz, dk].wait_recv()
+            far_copies[dz, dk].wait_recv()
+            slot = zslot(dz, dk)
+            got = jnp.concatenate([nbuf[slot, 0:15], fbuf[slot].astype(jnp.float32)[0:9]], axis=0)
+            part = got if part is None else part + got
+        turn = 3 * dz
+        if turn:
+            part = jnp.concatenate([part[turn:24], part[0:turn]], axis=0)
+        degree = degree + part
+    dinv[...] = lax.rsqrt(1.0 + degree * (1.0 / THETA))
+
+    for d in handed:
+        handed[d].wait_recv()
     for m, d in enumerate(ZORDER):
-        place = (z + d) % NZ
-        for t in range(3):
-            block = racc[PAIR * m + 128 * t:PAIR * m + 128 * (t + 1), :].T
-            dpart[pl.ds(place * 3 + t, 1), :] = jnp.sum(block, axis=0, keepdims=True)
-    copies = []
-    for p in zpeers:
-        s = zslot(*p)
-        copies.append(push(dpart, dbuf.at[s], 3, s, zdev(*p)))
-    degree = dpart[...]
-    for copy, p in zip(copies, zpeers):
-        copy.wait_recv()
-        degree = degree + dbuf[zslot(*p)]
-    dbuf[0] = lax.rsqrt(1.0 + degree * (1.0 / THETA))
-
-    for copy in bases:
-        copy.wait_recv()
-    for m, d in enumerate(ZORDER):
-        place = (z + d) % NZ
+        place = 3 * ((d + 2) % NZ)
         a, b = bbuf[2 * d].astype(jnp.float32), bbuf[2 * d + 1].astype(jnp.float32)
         pieces = (a[0:K], b[0:K], pair_tail(a[K:2 * K], b[K:2 * K]))
         for t, piece in enumerate(pieces):
-            row = dbuf[0, pl.ds(place * 3 + t, 1), :]
+            row = dinv[place + t:place + t + 1, :]
             scaled[:, PAIR * m + 128 * t:PAIR * m + 128 * (t + 1)] = (piece * row).astype(jnp.bfloat16)
 
     low = lax.broadcasted_iota(jnp.int32, (16, 128), 1) < 64
@@ -274,8 +318,8 @@
     low32 = lax.broadcasted_iota(jnp.int32, (K, 128), 1) < 64
     rest = held[32:48]
     rest = jnp.concatenate([rest, pltpu.roll(rest, 64, 1)], axis=0)
-    dmain = dbuf[0, pl.ds(z * 3 + k, 1), :]
-    dtail = dbuf[0, pl.ds(z * 3 + 2, 1), :]
+    dmain = dinv[pl.ds(6 + k, 1), :]
+    dtail = dinv[8:9, :]
     dtail = jnp.where(k == 0, dtail, pltpu.roll(dtail, 64, 1))
     img0 = held[0:32] * (dmain * (1.0 / THETA))
     img1 = jnp.where(low32, rest * (dtail * (1.0 / THETA)), 0.0)
@@ -306,11 +350,17 @@
     lane = lax.broadcasted_iota(jnp.int32, (K, 128), 1)
     sub = lax.broadcasted_iota(jnp.int32, (K, 128), 0)
     side = jnp.where(lane < 64, img1, pltpu.roll(jnp.where(lane < 32, gram, 0.0), 64, 1))
-    for j in range(K - 1):
-        pivot = side[j:j + 1, 64 + j:65 + j]
-        factor = jnp.where(sub > j, side[:, 64 + j:65 + j] * (1.0 / pivot), 0.0)
-        img0 = img0 - factor * img0[j:j + 1]
-        side = side - factor * side[j:j + 1]
+    for j in range(0, K, 2):
+        col_a = jnp.broadcast_to(side[:, 64 + j:65 + j], (K, 128))
+        col_b = jnp.broadcast_to(side[:, 65 + j:66 + j], (K, 128))
+        aa, ab, bb = col_a[j:j + 1], col_b[j:j + 1], col_b[j + 1:j + 2]
+        ra = 1.0 / aa
+        ratio = ab * ra
+        rest = 1.0 / (bb - ab * ratio)
+        fac_b = jnp.where(sub > j + 1, (col_b - col_a * ratio) * rest, 0.0)
+        fac_a = jnp.where(sub > j, col_a * ra - fac_b * ratio, 0.0)
+        img0 = img0 - (fac_a * img0[j:j + 1] + fac_b * img0[j + 1:j + 2])
+        side = side - (fac_a * side[j:j + 1] + fac_b * side[j + 1:j + 2])
     diag = jnp.sum(jnp.where(lane == sub + 64, side, 0.0), axis=1, keepdims=True)
     final = lax.rsqrt(diag) * math.sqrt(NPTS)
     out[:, 0:128] = img0 * final
@@ -324,9 +374,12 @@
     return pl.pallas_call(
         kernel,
         out_shape=jax.ShapeDtypeStruct((K, SEG), f32),
-        in_specs=[pl.BlockSpec(memory_space=pltpu.VMEM)] * 3,
+        in_specs=[pl.BlockSpec(memory_space=pl.ANY)] * 3,
         out_specs=pl.BlockSpec(memory_space=pltpu.VMEM),
         scratch_shapes=[
+            pltpu.VMEM((SEG, E), bf16),
+            pltpu.VMEM((1, SEG), jnp.int32),
+            pltpu.VMEM((K, SEG), bf16),
             pltpu.VMEM((16, XROWS, 128), bf16),
             pltpu.VMEM((16, XROWS, 128), bf16),
             pltpu.VMEM((16, 2 * K, 128), bf16),
@@ -336,8 +389,11 @@
             pltpu.VMEM((8, SIDE), f32),
             pltpu.VMEM((SIDE, SIDE), bf16),
             pltpu.VMEM((SIDE, 128), f32),
+            pltpu.VMEM((16, 128), f32),
+            pltpu.VMEM((16, 128), bf16),
+            pltpu.VMEM((16, 16, 128), f32),
+            pltpu.VMEM((16, 16, 128), bf16),
             pltpu.VMEM((24, 128), f32),
-            pltpu.VMEM((16, 24, 128), f32),
             pltpu.VMEM((K, SIDE), bf16),
             pltpu.VMEM((16, 48, 128), bf16),
             pltpu.VMEM((16, 48, 128), bf16),
@@ -345,8 +401,9 @@
             pltpu.VMEM((16, 8, 128), f32),
             pltpu.VMEM((8, 128), f32),
             pltpu.VMEM((16, 8, 128), f32),
-            pltpu.SemaphoreType.DMA((8, 16)),
-            pltpu.SemaphoreType.DMA((8, 16)),
+            pltpu.SemaphoreType.DMA((9, 16)),
+            pltpu.SemaphoreType.DMA((9, 16)),
+            pltpu.SemaphoreType.DMA((3,)),
         ],
         compiler_params=pltpu.CompilerParams(
             collective_id=0, has_side_effects=True, vmem_limit_bytes=60 * 2**20

time: 64.5 us -> 59.7 us (0.926)
  Pallas kernels: 63 us -> 58.2 us
    pallas_call x1, Pallas kernels: 63 us -> 58.2 us  [on_device(): pl.pallas_call(kernel, out_shape=jax.ShapeDtypeStruct((K, SEG), f32), in_...]
where the time goes in v4:
time: 59.7 us; the launch traced here: 59.5 us
  Pallas kernels  58.2 us (97%)
  local copies, waits for them, and re-layouts  1.38 us (2%)
    pallas_call x1, Pallas kernels, on_device(): pl.pallas_call(kernel, out_shape=jax.ShapeDtypeStruct((K, SEG), f32), in_...  58.2 us
    unnamed x1, local copies, waits for them, and re-layouts  1.38 us

profile of v4, /device:TPU:1, one launch (start us, length us, event | category | flops | bytes accessed | tf_op | source)
XLA Modules:
  0.0 59.5 jit_solution(15698904641948348155)
XLA Ops:
  0.0 58.2 %shard_map.37 = f32[32,192]{1,0:T(8,128)} custom-call(bf16[192,128]{1,0:T(8,128)(2,1)} %emb_hbm.1, s32[1,192]{1,0:T(1,128)} %bitcast.1, bf16[32,192]{1,0:T(8,128)(2,1)} %basis_hbm.1), custom_call_target="tpu_custom_call" | custom-call | tf_op jit(solution)/shard_map/pallas_call | solution.py:374
  58.2 1.4 %copy.5 = f32[32,192]{1,0:T(8,128)} copy(f32[32,192]{1,0:T(8,128)} %shard_map.37) | data formatting | bytes 49152

commit v5 on v4

--- a/solution.py
+++ b/solution.py
@@ -137,38 +137,6 @@
     plane[1, 0].wait_recv()
     for step in (1, -1, 2):
         phop(1, 0, 0, step)
-    hop[6].wait_recv()
-    zhop(6, 1)
-    hop[2].wait_recv()
-    zhop(2, -1)
-    turn = jnp.where(lead, 6, 2)
-    hop[4] = push(zblock(turn), zblock(4), 0, 4, zdev(jnp.where(lead, 2, NZ - 2), 0))
-    relay(6)
-    relay(2)
-    hop[7].wait_recv()
-    relay(7)
-    hop[1].wait_recv()
-    relay(1)
-    plane[0, 1].wait_recv()
-    phop(0, 1, 0, -1)
-    plane[2, 0].wait_recv()
-    for step in (1, -1, 2):
-        phop(2, 0, 0, step)
-    bases, handed = {}, {}
-
-    def basis_to(dz):
-        d = (NZ - dz) % NZ
-        bases[d] = push(bown, bbuf.at[2 * d + k], 7, d, zdev(dz, 0))
-
-    def basis_relay(d):
-        if d:
-            bases[d].wait_recv()
-        handed[d] = push(bbuf.at[2 * d + k], bbuf.at[2 * d + k], 7, 8 + d, zdev(0, 1))
-
-    for dz in (6, 2, 7, 1):
-        basis_to(dz)
-    seen = {(0, 0), (3, 0), (1, 0), (0, 1), (2, 0)}
-
     def lane_ids(buf, s):
         rows = buf[s, UROWS:XROWS].astype(jnp.float32)
         return rows[0:1] * 256.0 + rows[1:2], rows[2:3] * 256.0 + rows[3:4]
@@ -211,7 +179,7 @@
                 total = total + weights
             racc[part, :] = total
 
-    first, second = slice(0, 3 * PAIR), slice(3 * PAIR, 5 * PAIR)
+    first, second = slice(0, PAIR), slice(PAIR, 5 * PAIR)
     near, far = slice(0, 5 * PAIR), slice(5 * PAIR, 8 * PAIR)
 
     def take_plane(n):
@@ -221,12 +189,44 @@
         take_xy(2 * n)
         take_xy(2 * n + 1)
 
+    seen = {(0, 0), (3, 0), (1, 0)}
+    hop[7].wait_recv()
+    relay(7)
+    hop[1].wait_recv()
+    relay(1)
     xbuf[0] = own[...]
     take_plane(0)
-    for m in range(3):
-        take_z(m)
+    take_z(0)
     affinity(first, 0)
-    for m in (3, 4):
+    hop[6].wait_recv()
+    zhop(6, 1)
+    hop[2].wait_recv()
+    zhop(2, -1)
+    turn = jnp.where(lead, 6, 2)
+    hop[4] = push(zblock(turn), zblock(4), 0, 4, zdev(jnp.where(lead, 2, NZ - 2), 0))
+    relay(6)
+    relay(2)
+    plane[0, 1].wait_recv()
+    phop(0, 1, 0, -1)
+    plane[2, 0].wait_recv()
+    for step in (1, -1, 2):
+        phop(2, 0, 0, step)
+    bases, handed = {}, {}
+
+    def basis_to(dz):
+        d = (NZ - dz) % NZ
+        bases[d] = push(bown, bbuf.at[2 * d + k], 7, d, zdev(dz, 0))
+
+    def basis_relay(d):
+        if d:
+            bases[d].wait_recv()
+        handed[d] = push(bbuf.at[2 * d + k], bbuf.at[2 * d + k], 7, 8 + d, zdev(0, 1))
+
+    for dz in (6, 2, 7, 1):
+        basis_to(dz)
+    seen |= {(0, 1), (2, 0)}
+
+    for m in range(1, 5):
         take_z(m)
     affinity(second, 0)
     take_plane(1)
@@ -259,10 +259,11 @@
     near_copies = {p: push(dnear, nbuf.at[zslot(*p)], 3, zslot(*p), zdev(*p)) for p in zpeers}
 
     def body(n, carry):
-        affinity(far, n)
+        affinity(far, 2 * n)
+        affinity(far, 2 * n + 1)
         return carry
 
-    lax.fori_loop(0, 4, body, 0)
+    lax.fori_loop(0, 2, body, 0)
 
     sums = row_sums(range(5, 8))
     rest = jnp.concatenate([sums[row] for row in range(15, 24)] + [jnp.zeros((7, 128), jnp.float32)], axis=0)
@@ -406,7 +407,7 @@
             pltpu.SemaphoreType.DMA((3,)),
         ],
         compiler_params=pltpu.CompilerParams(
-            collective_id=0, has_side_effects=True, vmem_limit_bytes=60 * 2**20
+            collective_id=0, has_side_effects=True, vmem_limit_bytes=63 * 2**20
         ),
     )(embeddings, recordings.reshape(1, SEG), start_basis)
 

time: 59.7 us -> 58.7 us (0.983)
  Pallas kernels: 58.2 us -> 57.2 us
    pallas_call x1, Pallas kernels: 58.2 us -> 57.2 us  [on_device(): pl.pallas_call(kernel, out_shape=jax.ShapeDtypeStruct((K, SEG), f32), in_...]
where the time goes in v5:
time: 58.7 us; the launch traced here: 58.5 us
  Pallas kernels  57.2 us (97%)
  local copies, waits for them, and re-layouts  1.38 us (2%)
    pallas_call x1, Pallas kernels, on_device(): pl.pallas_call(kernel, out_shape=jax.ShapeDtypeStruct((K, SEG), f32), in_...  57.2 us
    unnamed x1, local copies, waits for them, and re-layouts  1.38 us

profile of v5, /device:TPU:1, one launch (start us, length us, event | category | flops | bytes accessed | tf_op | source)
XLA Modules:
  0.0 58.5 jit_solution(1754603236867625110)
XLA Ops:
  0.0 57.2 %shard_map.37 = f32[32,192]{1,0:T(8,128)} custom-call(bf16[192,128]{1,0:T(8,128)(2,1)} %emb_hbm.1, s32[1,192]{1,0:T(1,128)} %bitcast.1, bf16[32,192]{1,0:T(8,128)(2,1)} %basis_hbm.1), custom_call_target="tpu_custom_call" | custom-call | tf_op jit(solution)/shard_map/pallas_call | solution.py:375
  57.2 1.4 %copy.5 = f32[32,192]{1,0:T(8,128)} copy(f32[32,192]{1,0:T(8,128)} %shard_map.37) | data formatting | bytes 49152
